TPU v7x, 32 devices: a whole 2x2x4 slice. The times are simulated.
32 devices in a mesh: dp: 8 (over z, x), head: 4 (over y, core).
Axes of the slice: x: 2, y: 2, z: 4, core: 2. Of those that a mesh axis runs over, the one named last changes fastest.
Arguments:
- tokens: bfloat16 [64, 512, 768], P('dp', 'head'), may hold values from -6 to 6
- bucket_of_block: int32 [8, 8], P('dp'), may hold values from 0 to 2, as said below
- lengths: int32 [8, 8, 4], P('dp'), may hold values from 0 to 512, as said below
- w_query: bfloat16 [768, 768], replicated, may hold values from -0.109375 to 0.109375
- w_key: bfloat16 [768, 768], replicated, may hold values from -0.109375 to 0.109375
- w_value: bfloat16 [768, 768], replicated, may hold values from -0.21875 to 0.21875
- w_out: bfloat16 [768, 768], replicated, may hold values from -0.625 to 0.625
- w_in: bfloat16 [768, 3072], replicated, may hold values from -0.21875 to 0.21875
- w_back: bfloat16 [3072, 768], replicated, may hold values from -0.109375 to 0.109375
- gain_attn: float32 [768], replicated, may hold values from 0.5 to 1.5
- gain_ffn: float32 [768], replicated, may hold values from 0.5 to 1.5
- bias_table: float32 [32, 12], P(None, 'head'), may hold values from -4 to 4
- cotangent: bfloat16 [64, 512, 768], P('dp', 'head'), may hold values from -6 to 6
Outputs:
- output: bfloat16 [64, 512, 768], P('dp', 'head')
- grad_tokens: bfloat16 [64, 512, 768], P('dp', 'head')
- grad_w_query: float32 [768, 768], P('dp', 'head')
- grad_w_key: float32 [768, 768], P('dp', 'head')
- grad_w_value: float32 [768, 768], P('dp', 'head')
- grad_w_out: float32 [768, 768], P('dp', 'head')
- grad_w_in: float32 [768, 3072], P('dp', 'head')
- grad_w_back: float32 [3072, 768], P('dp', 'head')
- grad_gain_attn: float32 [768], P('head')
- grad_gain_ffn: float32 [768], P('head')
- grad_bias_table: float32 [32, 12], P(None, 'head')
Inputs may be any that keep to these rules, and one draw needn't show every extreme that they name: A block with bucket b holds 4 // 2**b documents of 512 // 4 * 2**b slots each; every row of bucket_of_block has one or more blocks with b = 2. `lengths`: entry s of a block is the real length of its document s for s < 4 // 2**b, between a quarter of the document's slots and all of them, and 0 for the other entries; every row has a block of bucket 2 that holds one document of exactly 512 tokens.
All inputs are finite; a program needn't handle non-finite values.
Results may differ from a plain program's by a relative error of at most 0.015.
Values may be sent and summed in bfloat16 or wider, within the bound.
A program may use at most 192 MiB of HBM per device.

v0:
```python
import jax
import jax.numpy as jnp
from jax import lax
from jax.sharding import PartitionSpec as P

HEADS = 12
HEAD_DIM = 64
BUCKETS = 32
BLOCK = 512


EPSILON = 1e-06


def rms_norm(values, gain):
    return values * lax.rsqrt(jnp.mean(values * values, axis=-1, keepdims=True) + EPSILON) * gain


def smooth_act(values):
    return jax.nn.gelu(values, approximate=True)


def rel_bucket(offset):
    direction_part = jnp.where(offset > 0, 16, 0).astype(jnp.int32)
    magnitude = jnp.abs(offset)
    far_bucket = jnp.full_like(magnitude, 8)
    for threshold in (12, 16, 23, 32, 46, 64, 91):
        far_bucket = far_bucket + (magnitude >= threshold).astype(jnp.int32)
    return direction_part + jnp.where(magnitude < 8, magnitude, far_bucket)


def block_masks(bucket_ids, seq_lengths):
    positions = jnp.arange(BLOCK, dtype=jnp.int32)
    span = (
        BLOCK
        // 4
        * jnp.where(bucket_ids == 0, 1, jnp.where(bucket_ids == 1, 2, 4)).astype(jnp.int32)
    )
    sequence = positions[None, :] // span[:, None]
    within = positions[None, :] % span[:, None]
    slots = jnp.arange(4, dtype=jnp.int32)
    key_length = jnp.sum(
        jnp.where(sequence[:, :, None] == slots, seq_lengths[:, None, :], 0), axis=-1
    )
    live_key = within < key_length
    return (sequence[:, :, None] == sequence[:, None, :]) & live_key[:, None, :]


def shards(
    tokens,
    bucket_of_block,
    lengths,
    w_query,
    w_key,
    w_value,
    w_out,
    w_in,
    w_back,
    gain_attn,
    gain_ffn,
    bias_table,
    cotangent,
):
    parts = lax.axis_size("head")
    local_heads = HEADS // parts
    local_width = local_heads * HEAD_DIM
    blocks_here, row_count, features = tokens.shape
    total_rows = blocks_here * row_count
    token_rows = tokens.astype(jnp.float32).reshape(total_rows, features)
    normed_float, attn_norm_back = jax.vjp(rms_norm, token_rows, gain_attn)
    normed_attn = normed_float.astype(jnp.bfloat16)
    query_rows, key_rows, value_rows = tuple(
        (
            jnp.dot(normed_attn, weight, preferred_element_type=jnp.float32)
            .astype(jnp.bfloat16)
            .reshape(blocks_here, row_count, features)
            for weight in (w_query, w_key, w_value)
        )
    )
    head_query, head_key, head_value = (
        lax.all_to_all(query_rows, "head", split_axis=2, concat_axis=1, tiled=True),
        lax.all_to_all(key_rows, "head", split_axis=2, concat_axis=1, tiled=True),
        lax.all_to_all(value_rows, "head", split_axis=2, concat_axis=1, tiled=True),
    )
    head_query, head_key, head_value = (head_query, head_key, head_value)
    valid_pairs = block_masks(bucket_of_block.reshape(-1), lengths.reshape(-1, 4))
    positions = jnp.arange(BLOCK, dtype=jnp.int32)
    onehot = (
        rel_bucket(positions[None, :] - positions[:, None])[:, :, None]
        == jnp.arange(BUCKETS, dtype=jnp.int32)
    ).astype(jnp.float32)
    position_bias = jnp.einsum("qkb,bh->hqk", onehot, bias_table, precision=lax.Precision.HIGHEST)

    def split_heads(values):
        return values.reshape(BLOCK, local_heads, HEAD_DIM)

    def scores_of(query_block, key_block, mask_block):
        scores = (
            jnp.einsum(
                "qhd,khd->hqk",
                split_heads(query_block),
                split_heads(key_block),
                preferred_element_type=jnp.float32,
            )
            + position_bias
        )
        return jnp.where(mask_block[None], scores, -1000000000.0)

    def attend(inputs):
        query_block, key_block, value_block, mask_block = inputs
        scores = scores_of(query_block, key_block, mask_block)
        peak_score = jnp.max(scores, axis=-1, keepdims=True)
        exp_scores = jnp.exp(scores - peak_score)
        totals = jnp.sum(exp_scores, axis=-1, keepdims=True)
        probabilities = exp_scores / totals
        context_block = jnp.einsum(
            "hqk,khd->qhd",
            probabilities.astype(jnp.bfloat16),
            split_heads(value_block),
            preferred_element_type=jnp.float32,
        )
        return (
            context_block.astype(jnp.bfloat16).reshape(BLOCK, local_width),
            (peak_score + jnp.log(totals))[:, :, 0],
        )

    context_heads, log_totals = lax.map(attend, (head_query, head_key, head_value, valid_pairs))
    context = lax.all_to_all(context_heads, "head", split_axis=1, concat_axis=2, tiled=True)
    context_rows = context.reshape(total_rows, features)
    hidden = token_rows + jnp.dot(context_rows, w_out, preferred_element_type=jnp.float32)
    normed_hidden, ffn_norm_back = jax.vjp(rms_norm, hidden, gain_ffn)
    normed_ffn = normed_hidden.astype(jnp.bfloat16)
    inner = jnp.dot(normed_ffn, w_in, preferred_element_type=jnp.float32)
    activated_float, act_back = jax.vjp(smooth_act, inner)
    activated = activated_float.astype(jnp.bfloat16)
    output = (
        (hidden + jnp.dot(activated, w_back, preferred_element_type=jnp.float32))
        .astype(jnp.bfloat16)
        .reshape(blocks_here, row_count, features)
    )
    grad_rows = cotangent.reshape(total_rows, features)
    grad_w_back = jnp.einsum("rf,rd->fd", activated, grad_rows, preferred_element_type=jnp.float32)
    grad_activated = jnp.einsum("rd,fd->rf", grad_rows, w_back, preferred_element_type=jnp.float32)
    grad_inner = act_back(grad_activated)[0].astype(jnp.bfloat16)
    grad_w_in = jnp.einsum("rd,rf->df", normed_ffn, grad_inner, preferred_element_type=jnp.float32)
    grad_normed_ffn = jnp.einsum("rf,df->rd", grad_inner, w_in, preferred_element_type=jnp.float32)
    grad_hidden_norm, grad_gain_ffn = ffn_norm_back(grad_normed_ffn)
    grad_hidden = grad_rows.astype(jnp.float32) + grad_hidden_norm
    grad_attn_out = grad_hidden.astype(jnp.bfloat16)
    grad_w_out = jnp.einsum(
        "rd,re->de", context_rows, grad_attn_out, preferred_element_type=jnp.float32
    )
    grad_context = (
        jnp.einsum("re,de->rd", grad_attn_out, w_out, preferred_element_type=jnp.float32)
        .astype(jnp.bfloat16)
        .reshape(blocks_here, row_count, features)
    )
    grad_heads = lax.all_to_all(grad_context, "head", split_axis=2, concat_axis=1, tiled=True)

    def attend_back(carry_sum, inputs):
        query_block, key_block, value_block, grad_block, mask_block, log_block = inputs
        scores = scores_of(query_block, key_block, mask_block)
        probabilities = jnp.exp(scores - log_block[:, :, None])
        grad_probs = jnp.einsum(
            "qhd,khd->hqk",
            split_heads(grad_block),
            split_heads(value_block),
            preferred_element_type=jnp.float32,
        )
        grad_scores = probabilities * (
            grad_probs - jnp.sum(probabilities * grad_probs, axis=-1, keepdims=True)
        )
        grad_value = jnp.einsum(
            "hqk,qhd->khd",
            probabilities.astype(jnp.bfloat16),
            split_heads(grad_block),
            preferred_element_type=jnp.float32,
        )
        scores_low = grad_scores.astype(jnp.bfloat16)
        grad_query = jnp.einsum(
            "hqk,khd->qhd", scores_low, split_heads(key_block), preferred_element_type=jnp.float32
        )
        grad_key = jnp.einsum(
            "hqk,qhd->khd", scores_low, split_heads(query_block), preferred_element_type=jnp.float32
        )
        merged = tuple(
            (
                part_grad.astype(jnp.bfloat16).reshape(BLOCK, local_width)
                for part_grad in (grad_query, grad_key, grad_value)
            )
        )
        return (carry_sum + grad_scores, merged)

    score_sum, head_grads = lax.scan(
        attend_back,
        jnp.zeros((local_heads, BLOCK, BLOCK), jnp.float32),
        (head_query, head_key, head_value, grad_heads, valid_pairs, log_totals),
    )
    grad_query_rows, grad_key_rows, grad_value_rows = (
        lax.all_to_all(head_grads[0], "head", split_axis=1, concat_axis=2, tiled=True),
        lax.all_to_all(head_grads[1], "head", split_axis=1, concat_axis=2, tiled=True),
        lax.all_to_all(head_grads[2], "head", split_axis=1, concat_axis=2, tiled=True),
    )
    query_grad_flat = grad_query_rows.reshape(total_rows, features)
    key_grad_flat = grad_key_rows.reshape(total_rows, features)
    value_grad_flat = grad_value_rows.reshape(total_rows, features)
    grad_w_query = jnp.einsum(
        "rd,re->de", normed_attn, query_grad_flat, preferred_element_type=jnp.float32
    )
    grad_w_key = jnp.einsum(
        "rd,re->de", normed_attn, key_grad_flat, preferred_element_type=jnp.float32
    )
    grad_w_value = jnp.einsum(
        "rd,re->de", normed_attn, value_grad_flat, preferred_element_type=jnp.float32
    )
    grad_normed_attn = (
        jnp.einsum("re,de->rd", query_grad_flat, w_query, preferred_element_type=jnp.float32)
        + jnp.einsum("re,de->rd", key_grad_flat, w_key, preferred_element_type=jnp.float32)
        + jnp.einsum("re,de->rd", value_grad_flat, w_value, preferred_element_type=jnp.float32)
    )
    grad_token_norm, grad_gain_attn = attn_norm_back(grad_normed_attn)
    grad_tokens = (
        (grad_hidden + grad_token_norm)
        .astype(jnp.bfloat16)
        .reshape(blocks_here, row_count, features)
    )
    grad_table_local = jnp.einsum("qkb,hqk->bh", onehot, score_sum, precision=lax.Precision.HIGHEST)
    row_sums = (
        lax.psum_scatter(grad_w_query, "dp", scatter_dimension=0, tiled=True),
        lax.psum_scatter(grad_w_key, "dp", scatter_dimension=0, tiled=True),
        lax.psum_scatter(grad_w_value, "dp", scatter_dimension=0, tiled=True),
        lax.psum_scatter(grad_w_out, "dp", scatter_dimension=0, tiled=True),
        lax.psum_scatter(grad_w_in, "dp", scatter_dimension=0, tiled=True),
        lax.psum_scatter(grad_w_back, "dp", scatter_dimension=0, tiled=True),
    )
    gain_attn_sum, gain_ffn_sum, table_sum = lax.psum(
        (grad_gain_attn, grad_gain_ffn, grad_table_local), "dp"
    )
    final_sums = (
        lax.psum_scatter(
            row_sums[0].astype(jnp.bfloat16), "head", scatter_dimension=1, tiled=True
        ).astype(jnp.float32),
        lax.psum_scatter(
            row_sums[1].astype(jnp.bfloat16), "head", scatter_dimension=1, tiled=True
        ).astype(jnp.float32),
        lax.psum_scatter(
            row_sums[2].astype(jnp.bfloat16), "head", scatter_dimension=1, tiled=True
        ).astype(jnp.float32),
        lax.psum_scatter(
            row_sums[3].astype(jnp.bfloat16), "head", scatter_dimension=1, tiled=True
        ).astype(jnp.float32),
        lax.psum_scatter(
            row_sums[4].astype(jnp.bfloat16), "head", scatter_dimension=1, tiled=True
        ).astype(jnp.float32),
        lax.psum_scatter(
            row_sums[5].astype(jnp.bfloat16), "head", scatter_dimension=1, tiled=True
        ).astype(jnp.float32),
        lax.psum_scatter(
            gain_attn_sum.astype(jnp.bfloat16), "head", scatter_dimension=0, tiled=True
        ).astype(jnp.float32),
        lax.psum_scatter(
            gain_ffn_sum.astype(jnp.bfloat16), "head", scatter_dimension=0, tiled=True
        ).astype(jnp.float32),
    )
    weight_sums = final_sums[:6]
    gain_attn_out = final_sums[6]
    gain_ffn_out = final_sums[7]
    return (
        output,
        grad_tokens,
        weight_sums[0],
        weight_sums[1],
        weight_sums[2],
        weight_sums[3],
        weight_sums[4],
        weight_sums[5],
        gain_attn_out,
        gain_ffn_out,
        table_sum,
    )


def solution(mesh):
    placed = (
        P("dp", "head", None),
        P("dp", None),
        P("dp", None, None),
        P(),
        P(),
        P(),
        P(),
        P(),
        P(),
        P(),
        P(),
        P(None, "head"),
        P("dp", "head", None),
    )
    return jax.shard_map(
        shards,
        mesh=mesh,
        in_specs=placed,
        out_specs=(
            P("dp", "head", None),
            P("dp", "head", None),
            P("dp", "head"),
            P("dp", "head"),
            P("dp", "head"),
            P("dp", "head"),
            P("dp", "head"),
            P("dp", "head"),
            P("head"),
            P("head"),
            P(None, "head"),
        ),
        check_vma=False,
    )
```

profile of v0, /device:TPU:0, one launch (start us, length us, event | category | flops | bytes accessed | tf_op | source)
XLA Modules:
  0.0 1175.1 jit_solution(9804690415373662196)
XLA Ops:
  29.9 11.5 all-to-all-done.2
  62.6 45.7 %copy.121 = pred[512,512,32]{1,2,0:T(32,128)(4,1)S(1)} copy(pred[512,512,32]{0,2,1:T(32,128)(4,1)} %iota_compare_fusion) | data formatting | bytes 16777216 | tf_op jit(solution)/shard_map/eq | solution.py:89
  108.3 10.1 convolution_bitcast_fusion
  153.7 59.8 %while.29 = (s32[]{:T(128)}, bf16[8,512,192]{1,2,0:T(8,128)(2,1)}, f32[8,3,512]{2,1,0:T(4,128)S(1)}, bf16[8,512,192]{1,2,0:T(8,128)(2,1)}, pred[8,512,512]{1,2,0...) while((s32[]{:T(128)}, bf16[8,512,192]{1,2,0:T(8,128)(2,1)}, ...), condition=%wide.region_5.6_spmd, body=%wide.region_2.5_spmd.sunk | while | flops 207714816 | bytes 15784057 | solution.py:127
  217.9 30.4 %all_to_all.132 = bf16[8,512,192]{2,0,1:T(8,128)(2,1)} all-to-all(bf16[8,512,192]{2,0,1:T(8,128)(2,1)} %copy.123), channel_id=1, replica_groups=mesh['dp'=8,'head'=4] {'head'}, dimensions={1} | all-to-all | bytes 3145728 | tf_op jit(solution)/shard_map/all_to_all | solution.py:128
  256.7 11.6 fusion.81
  268.4 15.4 %fusion.15 = bf16[1024,3072]{1,0:T(8,128)(2,1)} fusion(f32[1024,3072]{1,0:T(8,128)} %fusion.81, bf16[1024,768]{1,0:T(8,128)(2,1)S(1)} %bitcast.279, bf16[3072,768]{1,0:T(8,128)(2,1)S(1)} %bitcast.293), kind=kOutput, calls=%fused_computation.40 | convolution fusion | flops 4894752768 | bytes 25165824 | tf_op jit(solution)/shard_map/rd,fd->rf/dot_general | solution.py:143
  308.3 14.9 %all-to-all-done.4 = bf16[8,128,768]{1,0,2:T(8,128)(2,1)} async-done(((bf16[8,128,768]{1,0,2:T(8,128)(2,1)}), bf16[8,128,768]{1,0,2:T(8,128)(2,1)}, u32[]{:S(2)}, u32[]{:S(2)}) %all-to-all-start.4) | async-done | bytes 1572896 | tf_op jit(solution)/shard_map/all_to_all | solution.py:158
  334.5 104.4 %while.30 = (s32[]{:T(128)}, f32[3,512,512]{1,2,0:T(8,128)}, bf16[8,512,192]{1,2,0:T(8,128)(2,1)}, bf16[8,512,192]{1,2,0:T(8,128)(2,1)}, bf16[8,512,192]{1,2,0:T...) while((s32[]{:T(128)}, f32[3,512,512]{1,2,0:T(8,128)}, ...), condition=%wide.region_10.11_spmd.clone, body=%wide.region_8.10_spmd.clone.sunk | while | flops 512260608 | bytes 76314888 | solution.py:194
  449.5 24.1 %all-to-all-done.6 = bf16[8,512,192]{2,0,1:T(8,128)(2,1)} async-done(((bf16[8,512,192]{2,0,1:T(8,128)(2,1)}), bf16[8,512,192]{2,0,1:T(8,128)(2,1)}, u32[]{:S(2)}, u32[]{:S(2)}) %all-to-all-start.6) | async-done | bytes 1572896 | tf_op jit(solution)/shard_map/all_to_all | solution.py:201
  487.5 30.3 %all_to_all.133 = bf16[8,512,192]{2,0,1:T(8,128)(2,1)} all-to-all(bf16[8,512,192]{2,0,1:T(8,128)(2,1)} %copy.129), channel_id=1, replica_groups=mesh['dp'=8,'head'=4] {'head'}, dimensions={1} | all-to-all | bytes 3145728 | tf_op jit(solution)/shard_map/all_to_all | solution.py:200
  531.9 30.1 %all_to_all.134 = bf16[8,512,192]{2,0,1:T(8,128)(2,1)} all-to-all(bf16[8,512,192]{2,0,1:T(8,128)(2,1)} %copy.133), channel_id=1, replica_groups=mesh['dp'=8,'head'=4] {'head'}, dimensions={1} | all-to-all | bytes 3145728 | tf_op jit(solution)/shard_map/all_to_all | solution.py:202
  571.5 12.9 %fusion.82 = f32[3072,768]{1,0:T(8,128)} fusion(bf16[1024,768]{1,0:T(8,128)(2,1)} %bitcast.278, f32[1024,3072]{1,0:T(8,128)} %fusion.81), kind=kOutput, calls=%fused_computation.146 | convolution fusion | flops 4860149760 | bytes 23592960 | tf_op jit(solution)/shard_map/rf,rd->fd/dot_general | solution.py:142
  584.5 10.6 fusion.80
  599.0 26.1 %reduce-scatter.23.cloned.1.call-done = f32[96,768]{1,0:T(8,128)} async-done(((f32[768,768]{1,0:T(8,128)}), f32[96,768]{1,0:T(8,128)}) %reduce-scatter.23.cloned.1.call-update) | async-done | bytes 294928 | tf_op jit(solution)/shard_map/reduce_scatter | solution.py:229
  628.2 68.3 %reduce-scatter.27.cloned.1.call-done = f32[96,768]{1,0:T(8,128)} async-done(((f32[768,768]{1,0:T(8,128)}), f32[96,768]{1,0:T(8,128)}) %reduce-scatter.27.cloned.1.call-update) | async-done | bytes 294928 | tf_op jit(solution)/shard_map/reduce_scatter | solution.py:231
  698.4 13.0 %add_convert_fusion = bf16[1024,768]{1,0:T(8,128)(2,1)} fusion(f32[1024,768]{1,0:T(8,128)} %copy-done.6, bf16[3072,768]{1,0:T(8,128)(2,1)} %param.25, f32[1024,3072]{1,0:T(8,128)} %fusion.81), kind=kOutput, calls=%fused_computation.67 | convolution fusion | flops 4861722624 | bytes 22020096 | tf_op jit(solution)/shard_map/dot_general | solution.py:137
  711.3 151.1 %reduce-scatter.35.cloned.1.call-done = f32[384,768]{1,0:T(8,128)} async-done(((f32[3072,768]{1,0:T(8,128)}), f32[384,768]{1,0:T(8,128)}) %reduce-scatter.35.cloned.1.call-update) | async-done | bytes 1179664 | tf_op jit(solution)/shard_map/reduce_scatter | solution.py:234
  865.1 19.0 %fusion.51 = f32[32,3]{0,1:T(4,128)S(1)} fusion(f32[3,512,512]{1,2,0:T(8,128)} %get-tuple-element.124, s32[512,512]{0,1:T(8,128)} %fusion.54), kind=kOutput, calls=%fused_computation.98 | convolution fusion | flops 310378496 | bytes 4194688 | tf_op jit(solution)/shard_map/qkb,hqk->bh/dot_general | solution.py:227
  892.4 136.1 %reduce-scatter.31.cloned.1.call-done = f32[96,3072]{1,0:T(8,128)} async-done(((f32[768,3072]{1,0:T(8,128)}), f32[96,3072]{1,0:T(8,128)}) %reduce-scatter.31.cloned.1.call-update) | async-done | bytes 1179664 | tf_op jit(solution)/shard_map/reduce_scatter | solution.py:233
  1037.8 35.2 %all-reduce.2 = (bf16[768]{0:T(1024)(128)(2,1)S(1)}, bf16[768]{0:T(1024)(128)(2,1)S(1)}, f32[32,3]{0,1:T(4,128)}) all-reduce(f32[768]{0:T(1024)S(1)} %get-tuple-element.321, f32[768]{0:T(1024)S(1)} %get-tuple-element.319, f32[32,3]{0,1:T(4,128)S(1)} %fusion.51), channel_id=1, replica_groups=mesh['dp'=8,'head'=4] {'dp'}, use_global_device_ids=true, to_apply=%region_25.26 | all-reduce | flops 1632 | bytes 9984 | tf_op jit(solution)/shard_map/psum | solution.py:236
  1096.9 20.5 %reduce-scatter.41.cloned.1.call-done = bf16[192,96]{1,0:T(8,128)(2,1)} async-done(((bf16[768,96]{1,0:T(8,128)(2,1)}), bf16[192,96]{1,0:T(8,128)(2,1)}) %reduce-scatter.41.cloned.1.call-update) | async-done | bytes 36880
  1118.9 23.1 %reduce-scatter.45.cloned.1.call-done = bf16[192,384]{1,0:T(8,128)(2,1)} async-done(((bf16[768,384]{1,0:T(8,128)(2,1)}), bf16[192,384]{1,0:T(8,128)(2,1)}) %reduce-scatter.45.cloned.1.call-update) | async-done | bytes 147472
  1143.9 22.6 %reduce-scatter.33.cloned.1.call-done = bf16[96,768]{1,0:T(8,128)(2,1)} async-done(((bf16[96,3072]{1,0:T(8,128)(2,1)}), bf16[96,768]{1,0:T(8,128)(2,1)}) %reduce-scatter.33.cloned.1.call-update) | async-done | bytes 147472 | tf_op jit(solution)/shard_map/reduce_scatter | solution.py:252
  (394 shorter events, 396.3 us)
Async XLA Ops:
  7.2 48.5 %copy-start = (bf16[768,768]{1,0:T(8,128)(2,1)S(1)}, bf16[768,768]{1,0:T(8,128)(2,1)}, u32[]{:S(2)}) copy-start(bf16[768,768]{1,0:T(8,128)(2,1)} %param.22) | copy-start | bytes 3538948
  17.1 24.3 %all-to-all-start.2 = ((bf16[8,128,768]{1,0,2:T(8,128)(2,1)}), bf16[8,128,768]{1,0,2:T(8,128)(2,1)S(1)}, u32[]{:S(2)}, u32[]{:S(2)}) async-start(bf16[8,128,768]{1,0,2:T(8,128)(2,1)} %copy.118), calls=%async_computation.2 | async-start | bytes 3145728 | tf_op jit(solution)/shard_map/all_to_all | solution.py:82
  41.4 81.9 %all-to-all-start.1 = ((bf16[8,128,768]{1,0,2:T(8,128)(2,1)}), bf16[8,128,768]{1,0,2:T(8,128)(2,1)}, u32[]{:S(2)}, u32[]{:S(2)}) async-start(bf16[8,128,768]{1,0,2:T(8,128)(2,1)} %copy.115), calls=%async_computation.1 | async-start | bytes 3145728 | tf_op jit(solution)/shard_map/all_to_all | solution.py:81
  62.6 45.7 %copy-start.16 = (f32[32,3]{0,1:T(4,128)S(1)}, f32[32,3]{0,1:T(4,128)}, u32[]{:S(2)}) copy-start(f32[32,3]{0,1:T(4,128)} %param.28) | copy-start | bytes 1156
  123.3 24.5 %all-to-all-start = ((bf16[8,128,768]{1,0,2:T(8,128)(2,1)}), bf16[8,128,768]{1,0,2:T(8,128)(2,1)}, u32[]{:S(2)}, u32[]{:S(2)}) async-start(bf16[8,128,768]{1,0,2:T(8,128)(2,1)} %copy.112), calls=%async_computation | async-start | bytes 3145728 | tf_op jit(solution)/shard_map/all_to_all | solution.py:83
  217.9 35.1 %copy-start.4 = (bf16[8,128,768]{2,1,0:T(8,128)(2,1)S(1)}, bf16[8,128,768]{2,1,0:T(8,128)(2,1)}, u32[]{:S(2)}) copy-start(bf16[8,128,768]{2,1,0:T(8,128)(2,1)} %param.17) | copy-start | bytes 4718596
  256.6 34.8 %copy-start.6 = (f32[1024,768]{1,0:T(8,128)}, f32[1024,768]{1,0:T(8,128)S(1)}, u32[]{:S(2)}) copy-start(f32[1024,768]{1,0:T(8,128)S(1)} %get-tuple-element.383) | copy-start | bytes 9437188
  256.7 27.0 %slice-start = ((s8[4718592]{0:T(1024)(128)(4,1)}), s8[4194304]{0:T(1024)(128)(4,1)S(1)}, s32[]{:S(2)}) async-start(s8[4718592]{0:T(1024)(128)(4,1)} %bitcast.290), calls=%async_computation.32 | async-start | bytes 8388608
  298.7 24.5 %all-to-all-start.4 = ((bf16[8,128,768]{1,0,2:T(8,128)(2,1)}), bf16[8,128,768]{1,0,2:T(8,128)(2,1)}, u32[]{:S(2)}, u32[]{:S(2)}) async-start(bf16[8,128,768]{1,0,2:T(8,128)(2,1)} %copy.125), calls=%async_computation.4 | async-start | bytes 3145728 | tf_op jit(solution)/shard_map/all_to_all | solution.py:158
  303.1 292.2 %reduce-scatter.29.cloned.1.call-start = ((), (), s32[]{:S(2)}) async-start(), calls=%async_computation.23 | async-start | bytes 2654208 | tf_op jit(solution)/shard_map/reduce_scatter | solution.py:232
  443.4 30.3 %all-to-all-start.6 = ((bf16[8,512,192]{2,0,1:T(8,128)(2,1)}), bf16[8,512,192]{2,0,1:T(8,128)(2,1)}, u32[]{:S(2)}, u32[]{:S(2)}) async-start(bf16[8,512,192]{2,0,1:T(8,128)(2,1)} %copy.131), calls=%async_computation.6 | async-start | bytes 4194304 | tf_op jit(solution)/shard_map/all_to_all | solution.py:201
  447.8 149.3 %reduce-scatter.25.cloned.1.call-start = ((), (), s32[]{:S(2)}) async-start(), calls=%async_computation.21 | async-start | bytes 2654208 | tf_op jit(solution)/shard_map/reduce_scatter | solution.py:230
  483.0 142.1 %reduce-scatter.23.cloned.1.call-start = ((), (), s32[]{:S(2)}) async-start(), calls=%async_computation.20 | async-start | bytes 2654208 | tf_op jit(solution)/shard_map/reduce_scatter | solution.py:229
  527.4 169.1 %reduce-scatter.27.cloned.1.call-start = ((), (), s32[]{:S(2)}) async-start(), calls=%async_computation.22 | async-start | bytes 2654208 | tf_op jit(solution)/shard_map/reduce_scatter | solution.py:231
  571.5 291.0 %reduce-scatter.35.cloned.1.call-start = ((), (), s32[]{:S(2)}) async-start(), calls=%async_computation.26 | async-start | bytes 10616832 | tf_op jit(solution)/shard_map/reduce_scatter | solution.py:234
  584.5 444.0 %reduce-scatter.31.cloned.1.call-start = ((), (), s32[]{:S(2)}) async-start(), calls=%async_computation.24 | async-start | bytes 10616832 | tf_op jit(solution)/shard_map/reduce_scatter | solution.py:233
  595.2 31.8 %copy-start.22 = (u32[32]{0:T(128)S(1)}, u32[32]{0:T(128)}, u32[]{:S(2)}) copy-start(u32[32]{0:T(128)} %constant.115) | copy-start | bytes 388
  595.2 488.9 %reduce-scatter.43.cloned.1.call-start = ((), (), s32[]{:S(2)}) async-start(), calls=%async_computation.30 | async-start | bytes 245760
  597.1 488.6 %reduce-scatter.39.cloned.1.call-start = ((), (), s32[]{:S(2)}) async-start(), calls=%async_computation.28 | async-start | bytes 245760
  599.0 496.3 %reduce-scatter.37.cloned.1.call-start = ((), (), s32[]{:S(2)}) async-start(), calls=%async_computation.27 | async-start | bytes 245760
  626.9 490.5 %reduce-scatter.41.cloned.1.call-start = ((), (), s32[]{:S(2)}) async-start(), calls=%async_computation.29 | async-start | bytes 245760
  698.3 443.7 %reduce-scatter.45.cloned.1.call-start = ((), (), s32[]{:S(2)}) async-start(), calls=%async_computation.31 | async-start | bytes 737280
  864.9 301.6 %reduce-scatter.33.cloned.1.call-start = ((), (), s32[]{:S(2)}) async-start(), calls=%async_computation.25 | async-start | bytes 737280 | tf_op jit(solution)/shard_map/reduce_scatter | solution.py:252
  889.2 141.5 %copy-start.12 = (f32[1024]{0:T(1024)S(1)}, f32[1024]{0:T(1024)}, u32[]{:S(2)}) copy-start(f32[1024]{0:T(1024)} %copy-done.11) | copy-start | bytes 12292
  (41 other events, 190.8 us)
Sparse Core Ops, SparseCore 0:
  308.4 71.4 reduce-scatter.28
  483.2 70.4 reduce-scatter.24
  557.1 67.9 reduce-scatter.22
  628.4 68.0 reduce-scatter.26
  699.9 162.4 reduce-scatter.34
  865.9 162.5 reduce-scatter.30
  1030.9 18.8 reduce-scatter.42
  1052.8 19.7 reduce-scatter.38
  1075.6 19.6 reduce-scatter.36
  1097.6 19.7 reduce-scatter.40
  1119.9 22.0 reduce-scatter.44
  1144.3 22.0 reduce-scatter.32
where the time goes:
time: 1180 us
  waiting for transfers between devices  513 us (43%)
  local copies, waits for them, and re-layouts  229 us (19%)
  matrix products  207 us (18%)
  blocking collectives  132 us (11%)
  other arithmetic  55.9 us (5%)
  starting transfers between devices  22.8 us (2%)
  between operations  15.4 us (1%)
    reduce_scatter x1, waiting for transfers between devices, shards(): lax.psum_scatter(grad_w_back, 'dp', scatter_dimension=0, tiled=True)  151 us
    reduce_scatter x1, waiting for transfers between devices, shards(): lax.psum_scatter(grad_w_in, 'dp', scatter_dimension=0, tiled=True)  136 us
    reduce_scatter x1, waiting for transfers between devices, shards(): lax.psum_scatter(grad_w_value, 'dp', scatter_dimension=0, tiled=True)  68.3 us
    unnamed x17, waiting for transfers between devices  51.9 us
    dynamic_slice x48, local copies, waits for them, and re-layouts, shards(): lax.map(attend, (head_query, head_key, head_value, valid_pairs))  47.4 us
    eq x1, local copies, waits for them, and re-layouts, shards(): rel_bucket(positions[None, :] - positions[:, None])[:, :, None]  45.7 us
    psum x1, blocking collectives, shards(): lax.psum((grad_gain_attn, grad_gain_ffn, grad_table_local), 'dp')  35.2 us
    dot_general x16, matrix products, scores_of(): jnp.einsum('qhd,khd->hqk', split_heads(query_block), split_heads(key_bloc...  31.6 us
  transfers between devices with their start and end apart: 17, of which 12 were waited for; matrix products, arithmetic and copies ran while one was open for 29% of the time, Pallas kernels for 0%

commit v1 on v0

v1 whole, which is shorter than its diff:
```python
import functools
import math

import jax
import jax.numpy as jnp
from jax import lax
from jax.experimental import pallas as pl
from jax.experimental.pallas import tpu as pltpu
from jax.sharding import PartitionSpec as P

D = 768
HEADS = 12
FF = 3072
BUCKETS = 32
BLOCK = 512
PAIRS = 6
OWN = 2
GROUP = 4
ROWS = 8
EPSILON = 1e-06
TILE = 128
MASKED = -1000000000.0
GELU_A = math.sqrt(2.0 / math.pi)
GELU_B = 0.044715

bf16 = jnp.bfloat16
f32 = jnp.float32
MESH = pl.DeviceIdType.MESH
ANY = pl.BlockSpec(memory_space=pl.ANY)
VMEM = pl.BlockSpec(memory_space=pltpu.VMEM)
SMEM = pl.BlockSpec(memory_space=pltpu.SMEM)
DMA = pltpu.SemaphoreType.DMA
STEPS = 3


def nn(left, right):
    return jnp.dot(left, right, preferred_element_type=f32)


def nt(left, right):
    return lax.dot_general(left, right, (((1,), (1,)), ((), ())), preferred_element_type=f32)


def tn(left, right):
    return lax.dot_general(left, right, (((0,), (0,)), ((), ())), preferred_element_type=f32)


def flat(ref, lanes=slice(None)):
    value = ref[:, :, lanes]
    return value.reshape(value.shape[0] * value.shape[1], value.shape[2])


def head_masks():
    lane = lax.broadcasted_iota(jnp.int32, (1, TILE), 1)
    low = (lane < TILE // 2).astype(f32)
    return low.astype(bf16), (1.0 - low).astype(bf16)


def bucket_of(offset):
    magnitude = jnp.abs(offset)
    far = jnp.full(offset.shape, 8, jnp.int32)
    for threshold in (12, 16, 23, 32, 46, 64, 91):
        far = far + (magnitude >= threshold).astype(jnp.int32)
    side = jnp.where(offset > 0, 16, 0).astype(jnp.int32)
    return side + jnp.where(magnitude < 8, magnitude, far)


def skew_offsets(tile):
    lane = lax.broadcasted_iota(jnp.int32, (1, 2 * TILE), 1)
    return TILE * tile + jnp.where(lane < TILE, -lane, 2 * TILE - lane)


def attend_kernel(
    tokens, cot, table, w_q, w_k, w_v, gain, buckets, lengths,
    x_out, cot_out, n_out, q_out, k_out, v_out, ctx_out, p_out,
    xs, ns, qs, ks, vs, cs, ps, wq, wk, wv, tabs, tiles, mask,
    own_sem, send_sem, recv_sem, cot_own, cot_send, cot_recv, tab_send, tab_recv, w_sem, out_sem, p_sem,
):
    me = lax.axis_index("head")
    y, c = me // 2, me % 2
    peers = ((1 - y) * 2 + c, (1 - y) * 2 + (1 - c), y * 2 + (1 - c))
    barrier = pltpu.get_barrier_semaphore()
    for peer in peers:
        pl.semaphore_signal(barrier, inc=1, device_id={"head": peer}, device_id_type=MESH)

    def mine(start):
        return pl.ds(pl.multiple_of(start * TILE, TILE), TILE)

    locals_ = []
    for blk in range(OWN):
        copy = pltpu.make_async_copy(tokens.at[me + GROUP * blk], xs.at[blk, mine(me)], own_sem.at[blk])
        copy.start()
        locals_.append(copy)
    weights = []
    for at, (src, dst) in enumerate(((w_q, wq), (w_k, wk), (w_v, wv))):
        copy = pltpu.make_async_copy(src, dst, w_sem.at[at])
        copy.start()
        weights.append(copy)
    own_cot = []
    for blk in range(OWN):
        copy = pltpu.make_async_copy(cot.at[me + GROUP * blk], cot_out.at[blk, mine(me)], cot_own.at[blk])
        copy.start()
        own_cot.append(copy)

    tabs[me] = table[...]
    pl.semaphore_wait(barrier, len(peers))

    def send(source, dest, sends, recvs, blk, at):
        return pltpu.make_async_remote_copy(
            src_ref=source.at[peers[at] + GROUP * blk],
            dst_ref=dest.at[blk, mine(me)],
            send_sem=sends.at[blk, at],
            recv_sem=recvs.at[blk, at],
            device_id={"head": peers[at]},
            device_id_type=MESH,
        )

    moves = [[send(tokens, xs, send_sem, recv_sem, blk, at) for at in range(3)] for blk in range(OWN)]
    cot_moves = [[send(cot, cot_out, cot_send, cot_recv, blk, at) for at in range(3)] for blk in range(OWN)]
    tab_moves = [
        pltpu.make_async_remote_copy(
            src_ref=table,
            dst_ref=tabs.at[me],
            send_sem=tab_send.at[at],
            recv_sem=tab_recv.at[at],
            device_id={"head": peers[at]},
            device_id_type=MESH,
        )
        for at in range(3)
    ]
    for at in range(3):
        moves[0][at].start()
    for at in range(3):
        tab_moves[at].start()
    for at in range(3):
        moves[1][at].start()

    key = lax.broadcasted_iota(jnp.int32, (BLOCK, BLOCK), 0)
    query = lax.broadcasted_iota(jnp.int32, (1, BLOCK), 1)
    for blk in range(OWN):
        block = me + GROUP * blk
        bucket = buckets[0, block]
        span = TILE * jnp.where(bucket == 0, 1, jnp.where(bucket == 1, 2, 4))
        start = jnp.zeros((1, BLOCK), jnp.int32)
        end = jnp.zeros((1, BLOCK), jnp.int32)
        for slot in range(4):
            inside = query >= slot * span
            start = jnp.where(inside, slot * span, start)
            end = jnp.where(inside, slot * span + lengths[0, block, slot], end)
        mask[blk] = jnp.where((key >= start) & (key < end), 0.0, MASKED).astype(f32)

    for copy in tab_moves:
        copy.wait()
    bucket_rows = [bucket_of(skew_offsets(tile)) for tile in (-1, 0, 1)]
    for group in range(GROUP):
        rows = tabs[group]
        for tile in range(3):
            values = jnp.zeros((8, 2 * TILE), f32)
            for bucket in range(BUCKETS):
                values = jnp.where(bucket_rows[tile] == bucket, rows[:, bucket : bucket + 1], values)
            for at in range(3):
                wide = jnp.broadcast_to(values[at : at + 1], (TILE, 2 * TILE))
                wide = pltpu.roll(wide, 0, 1, stride=1, stride_axis=0)
                tiles[3 * group + at, 1 + tile] = wide[:, :TILE]
        for at in range(3):
            tiles[3 * group + at, 0] = jnp.broadcast_to(rows[at : at + 1, 15:16], (TILE, TILE))
            tiles[3 * group + at, 4] = jnp.broadcast_to(rows[at : at + 1, 31:32], (TILE, TILE))

    def project(blk, half):
        rows = pl.ds(pl.multiple_of(half * 256, 256), 256)
        x = xs[blk, rows, :].astype(f32)
        r = lax.rsqrt(jnp.mean(x * x, axis=-1, keepdims=True) + EPSILON)
        normed = (x * r * gain[...]).astype(bf16)
        ns[blk, rows, :] = normed
        qs[blk, rows, :] = nn(normed, wq[...]).astype(bf16)
        ks[blk, rows, :] = nn(normed, wk[...]).astype(bf16)
        vs[blk, rows, :] = nn(normed, wv[...]).astype(bf16)

    for copy in weights:
        copy.wait()
    for blk in range(OWN):
        locals_[blk].wait()
        moves[blk][2].wait()
        project(blk, y)

    low, high = head_masks()
    drains = []

    def drain(src, dst, at):
        copy = pltpu.make_async_copy(src, dst, out_sem.at[at])
        copy.start()
        drains.append(copy)

    for blk in range(OWN):
        moves[blk][0].wait()
        moves[blk][1].wait()
        for copy in cot_moves[blk]:
            copy.start()
        project(blk, 1 - y)
        for at, (src, dst) in enumerate(((xs, x_out), (ns, n_out), (qs, q_out), (ks, k_out), (vs, v_out))):
            drain(src.at[blk], dst.at[blk], 5 * blk + at)

        def attend(pair, carry):
            lanes = pl.ds(pl.multiple_of(pair * TILE, TILE), TILE)
            q, k, v = qs[blk, :, lanes], ks[blk, :, lanes], vs[blk, :, lanes]
            slot = blk * PAIRS + pair
            total = None
            for e, sel in enumerate((low, high)):
                scores = nt(k, q * sel)
                head = 2 * pair + e
                for qt in range(4):
                    at_q = slice(TILE * qt, TILE * qt + TILE)
                    parts = []
                    for kt in range(4):
                        at_k = slice(TILE * kt, TILE * kt + TILE)
                        kind = min(max(kt - qt, -2), 2) + 2
                        parts.append(scores[at_k, at_q] + tiles[head, kind] + mask[blk, at_k, at_q])
                    peak = parts[0]
                    for part in parts[1:]:
                        peak = jnp.maximum(peak, part)
                    peak = jnp.max(peak, axis=0, keepdims=True)
                    parts = [jnp.exp(part - peak) for part in parts]
                    whole = parts[0] + parts[1] + parts[2] + parts[3]
                    scale = 1.0 / jnp.sum(whole, axis=0, keepdims=True)
                    for kt in range(4):
                        ps[slot, e, TILE * kt : TILE * kt + TILE, at_q] = (parts[kt] * scale).astype(bf16)
                part = tn(ps[slot, e], v * sel)
                total = part if total is None else total + part
            cs[blk, :, lanes] = total.astype(bf16)
            pltpu.make_async_copy(ps.at[slot], p_out.at[slot], p_sem.at[slot]).start()
            return carry

        lax.fori_loop(0, PAIRS, attend, 0)
        drain(cs.at[blk], ctx_out.at[blk], 10 + blk)

    for slot in range(OWN * PAIRS):
        pltpu.make_async_copy(ps.at[slot], p_out.at[slot], p_sem.at[slot]).wait()
    for copy in drains:
        copy.wait()
    for blk in range(OWN):
        own_cot[blk].wait()
        for copy in cot_moves[blk]:
            copy.wait()


def attend_call(tokens, cot, table, w_q, w_k, w_v, gain, buckets, lengths):
    rows = jax.ShapeDtypeStruct((OWN, BLOCK, D), bf16)
    probs = jax.ShapeDtypeStruct((OWN * PAIRS, 2, BLOCK, BLOCK), bf16)
    block_rows = pltpu.VMEM((OWN, BLOCK, D), bf16)
    square = pltpu.VMEM((D, D), bf16)
    return pl.pallas_call(
        attend_kernel,
        out_shape=(rows,) * 7 + (probs,),
        in_specs=[ANY, ANY, VMEM, ANY, ANY, ANY, VMEM, SMEM, SMEM],
        out_specs=(ANY,) * 8,
        scratch_shapes=[block_rows] * 6
        + [pltpu.VMEM(probs.shape, bf16), square, square, square]
        + [
            pltpu.VMEM((GROUP, 8, TILE), f32),
            pltpu.VMEM((HEADS, 5, TILE, TILE), f32),
            pltpu.VMEM((OWN, BLOCK, BLOCK), f32),
            DMA((OWN,)), DMA((OWN, 3)), DMA((OWN, 3)),
            DMA((OWN,)), DMA((OWN, 3)), DMA((OWN, 3)),
            DMA((3,)), DMA((3,)), DMA((3,)), DMA((12,)), DMA((OWN * PAIRS,)),
        ],
        compiler_params=pltpu.CompilerParams(collective_id=0, has_side_effects=True, vmem_limit_bytes=60 * 2**20),
    )(tokens, cot, table, w_q, w_k, w_v, gain, buckets, lengths)


AXES = ("x", "z0", "y", "z1")
ORDERS = (("x", "y", "z0", "z1"), ("z0", "x", "y", "z1"))
UNIT = (2, 2, 2, 2, 96, TILE)


def rest_kernel(
    outer,
    x_in, cot_in, n_in, q_in, k_in, v_in, ctx_in, p_in, w_q, w_k, w_v, w_o, w_in, w_back, gain_a, gain_f,
    output, grad_tokens, g_qkvo, g_in, g_back, g_small,
    xs, cots, ns, cs, hidden, total, back, dcs, wo, own,
    c_ffn, c_att, r0_ffn, r1_ffn, r2_ffn, r3_ffn, r0_att, r1_att, r2_att, r3_att,
    f_ffn, f_att, rf_ffn, rf_att, small, small_in, buckets_acc,
    in_sem, cs_send, cs_recv, ca_send, ca_recv, st_send, st_recv, fx_send, fx_recv, sm_send, sm_recv,
    out_own, out_send, out_recv,
):
    me = lax.axis_index("head")
    dp = lax.axis_index("dp")
    y, c = me // 2, me % 2
    chunk, spare = dp // outer, dp % outer
    z1, z0, x = chunk // 4, (chunk // 2) % 2, chunk % 2
    place = {"x": x, "y": y, "z0": z0, "z1": z1}

    def device(row, column):
        return {"dp": row * outer + spare, "head": column}

    partner = {
        "c": device(chunk, 2 * y + (1 - c)),
        "y": device(chunk, 2 * (1 - y) + c),
        "x": device(chunk + 1 - 2 * x, me),
        "z0": device(chunk + 2 - 4 * z0, me),
        "z1": device(chunk + 4 - 8 * z1, me),
    }
    peers = ((1 - y) * 2 + c, (1 - y) * 2 + (1 - c), y * 2 + (1 - c))
    greeted = [partner[axis] for axis in ("c", "y", "x", "z0", "z1")] + [{"head": peers[1]}]
    barrier = pltpu.get_barrier_semaphore()
    for other in greeted:
        pl.semaphore_signal(barrier, inc=1, device_id=other, device_id_type=MESH)

    loads = []
    for at, (src, dst) in enumerate(((ctx_in, cs), (w_o, wo), (x_in, xs), (cot_in, cots), (n_in, ns))):
        copy = pltpu.make_async_copy(src, dst, in_sem.at[at])
        copy.start()
        loads.append(copy)

    pl.semaphore_wait(barrier, len(greeted))

    def remote(src, dst, sends, recvs, other):
        return pltpu.make_async_remote_copy(
            src_ref=src, dst_ref=dst, send_sem=sends, recv_sem=recvs, device_id=other, device_id_type=MESH
        )

    def ffn_base(item, kind):
        return (item * 2 + kind) * 4

    def core_copies(item):
        if item < STEPS:
            copies = [
                remote(own.at[pl.ds(ffn_base(item, 1 - c), 4)], c_ffn.at[item], cs_send.at[item], cs_recv.at[item], partner["c"])
            ]
        else:
            g = item - STEPS
            copies = [
                remote(
                    own.at[ffn_base(g, 1 - c) + 2 * half + (1 - c)], c_att.at[g, half],
                    ca_send.at[g, half], ca_recv.at[g, half], partner["c"],
                )
                for half in range(2)
            ]
        return copies

    def add_into(target, arrived):
        target[...] = target[...] + arrived[...]

    def core_finish(item):
        for copy in core_copies(item):
            copy.wait()
        if item < STEPS:
            base = ffn_base(item, c)

            def add(at, carry):
                for b in range(2):
                    add_into(own.at[base + at, b], c_ffn.at[item, at, b])
                return carry

            lax.fori_loop(0, 4, add, 0)
        else:
            g = item - STEPS
            for half in range(2):
                slot = ffn_base(g, 1 - c) + 2 * half + c

                def add(b, carry):
                    add_into(own.at[slot, b], c_att.at[g, half, b])
                    return carry

                lax.fori_loop(0, 2, add, 0)

    def part(item, half, done, axis=None, value=None):
        index = []
        for name in ("z1", "z0", "x", "y"):
            if name == axis:
                index.append(value)
            elif name in done:
                index.append(place[name])
            else:
                index.append(slice(None))
        if item < STEPS:
            lead = pl.ds(ffn_base(item, c) + 2 * half, 2)
        else:
            lead = ffn_base(item - STEPS, 1 - c) + 2 * half + c
        return own.at[tuple([lead] + index)]

    stage_ffn = (r0_ffn, r1_ffn, r2_ffn, r3_ffn)
    stage_att = (r0_att, r1_att, r2_att, r3_att)

    def arrived_at(item, half, stage):
        if item < STEPS:
            return stage_ffn[stage].at[item, half]
        return stage_att[stage].at[item - STEPS, half]

    def stage_copies(item, stage):
        copies = []
        for half in range(2):
            order = ORDERS[half]
            axis = order[stage]
            copy = remote(
                part(item, half, order[:stage], axis, 1 - place[axis]), arrived_at(item, half, stage),
                st_send.at[item, half, stage], st_recv.at[item, half, stage], partner[axis],
            )
            copies.append(copy)
        return copies

    def stage_finish(item, stage):
        copies = stage_copies(item, stage)
        for half in range(2):
            copies[half].wait()
            order = ORDERS[half]
            kept = part(item, half, order[: stage + 1])
            arrived = arrived_at(item, half, stage)
            if stage < 3:
                add_into(kept, arrived)
            elif item < STEPS:
                f_ffn[item, half] = kept[...] + arrived[...]
            else:
                f_att[item - STEPS, half] = kept[...] + arrived[...]

    def fix_copies(item):
        if item < STEPS:
            copy = remote(f_ffn.at[item, 1 - c], rf_ffn.at[item], fx_send.at[item], fx_recv.at[item], partner["c"])
        else:
            g = item - STEPS
            copy = remote(f_att.at[g], rf_att.at[g], fx_send.at[item], fx_recv.at[item], partner["c"])
        return [copy]

    state = {}

    def advance(item):
        at = state.get(item, 0)
        state[item] = min(at + 1, 7)
        if at == 1:
            core_finish(item)
        elif 2 <= at < 6:
            stage_finish(item, at - 2)
        if at == 0:
            copies = core_copies(item)
        elif at < 5:
            copies = stage_copies(item, at - 1)
        elif at < 7:
            copies = fix_copies(item)
        else:
            copies = []
        for copy in copies:
            if at == 6:
                copy.wait()
            else:
                copy.start()

    for copy in loads[:3]:
        copy.wait()

    def project_out(at, carry):
        blk, half = at // 2, at % 2
        rows = pl.ds(pl.multiple_of(half * 256, 256), 256)
        hidden[blk, rows, :] = xs[blk, rows, :].astype(f32) + nn(cs[blk, rows, :], wo[...])
        return carry

    lax.fori_loop(0, 4, project_out, 0)

    def feed_forward(nf, act, dinner, win, wback, w_sem):
        def fetch(step):
            slot = step % 2
            copies = []
            for f in range(8):
                at = f * (FF // 8) + step * TILE
                into = pl.ds(f * TILE, TILE)
                copies.append(pltpu.make_async_copy(w_in.at[:, pl.ds(at, TILE)], win.at[slot, :, into], w_sem.at[slot, 0, f]))
                copies.append(pltpu.make_async_copy(w_back.at[pl.ds(at, TILE)], wback.at[slot, into], w_sem.at[slot, 1, f]))
            for copy in copies:
                copy.start()
            return copies

        fetched = [fetch(0), fetch(1)]

        def norm(at, carry):
            blk, half = at // 2, at % 2
            rows = pl.ds(pl.multiple_of(half * 256, 256), 256)
            h = hidden[blk, rows, :]
            r = lax.rsqrt(jnp.mean(h * h, axis=-1, keepdims=True) + EPSILON)
            nf[blk, rows, :] = (h * r * gain_f[...]).astype(bf16)
            return carry

        lax.fori_loop(0, 4, norm, 0)
        loads[3].wait()

        for step in range(STEPS):
            slot = step % 2
            for copy in fetched[step]:
                copy.wait()

            def rows_of(at, carry):
                blk, half = at // 2, at % 2
                rows = pl.ds(pl.multiple_of(half * 256, 256), 256)
                v = nn(nf[blk, rows, :], win[slot])
                square = v * v
                t = jnp.tanh(GELU_A * v * (1.0 + GELU_B * square))
                a = (0.5 * v * (1.0 + t)).astype(bf16)
                slope = 0.5 * (1.0 + t) + 0.5 * GELU_A * v * (1.0 - t * t) * (1.0 + 3.0 * GELU_B * square)
                act[blk, rows, :] = a
                g = (nt(cots[blk, rows, :], wback[slot]) * slope).astype(bf16)
                dinner[blk, rows, :] = g
                onward = nn(a, wback[slot])
                backward = nt(g, win[slot])
                if step == 0:
                    total[blk, rows, :] = hidden[blk, rows, :] + onward
                    back[blk, rows, :] = backward
                else:
                    total[blk, rows, :] += onward
                    back[blk, rows, :] += backward
                return carry

            lax.fori_loop(0, 4, rows_of, 0)
            if step >= 1:
                advance(step - 1)
            if step >= 2:
                advance(step - 2)
            if step + 2 < STEPS:
                fetched.append(fetch(step + 2))
            for b in range(2):
                res = tn(flat(nf), flat(dinner, slice(512 * b, 512 * b + 512))).astype(bf16)
                for m in range(4):
                    own[ffn_base(step, 0) + m, :, :, :, b] = res[:, TILE * m : TILE * m + TILE].reshape(2, 2, 2, 96, TILE)
            for b in range(2):
                res = tn(flat(cots, slice(384 * b, 384 * b + 384)), flat(act)).astype(bf16)
                for m in range(4):
                    for f in range(8):
                        own[ffn_base(step, 1) + m, f // 4, (f // 2) % 2, f % 2, b] = res[
                            96 * m : 96 * m + 96, TILE * f : TILE * f + TILE
                        ]
            advance(step)

    pl.run_scoped(
        feed_forward,
        nf=pltpu.VMEM((OWN, BLOCK, D), bf16),
        act=pltpu.VMEM((OWN, BLOCK, 1024), bf16),
        dinner=pltpu.VMEM((OWN, BLOCK, 1024), bf16),
        win=pltpu.VMEM((2, D, 1024), bf16),
        wback=pltpu.VMEM((2, 1024, D), bf16),
        w_sem=DMA((2, 2, 8)),
    )

    def send_back(rows_of, result, at_blk, sems_at):
        copies = []
        for at in range(3):
            copies.append(
                remote(
                    rows_of.at[at_blk, pl.ds(pl.multiple_of(peers[at] * TILE, TILE), TILE)],
                    result.at[me + GROUP * at_blk],
                    out_send.at[sems_at, at_blk, at], out_recv.at[sems_at, at_blk, at], {"head": peers[at]},
                )
            )
        copies.append(
            pltpu.make_async_copy(
                rows_of.at[at_blk, pl.ds(pl.multiple_of(me * TILE, TILE), TILE)],
                result.at[me + GROUP * at_blk], out_own.at[sems_at, at_blk],
            )
        )
        return copies

    def start_back(rows_of, result, at_blk, sems_at):
        for copy in send_back(rows_of, result, at_blk, sems_at):
            copy.start()

    def wait_back(rows_of, result, sems_at):
        for blk in range(OWN):
            for copy in send_back(rows_of, result, blk, sems_at):
                copy.wait()

    small[0] = jnp.zeros((32, TILE), f32)
    buckets_acc[...] = jnp.zeros_like(buckets_acc)

    def attention(qs, ks, vs, ps, dsb, acc, wq, wk, wv, l_sem, p_sem):
        more = []
        for at, (src, dst) in enumerate(((q_in, qs), (k_in, ks), (v_in, vs), (w_q, wq), (w_k, wk), (w_v, wv))):
            copy = pltpu.make_async_copy(src, dst, l_sem.at[at])
            copy.start()
            more.append(copy)

        def index_of(n):
            group, within = n // 4, n % 4
            return (within % 2) * PAIRS + group + 3 * (within // 2)

        def probs_copy(n):
            return pltpu.make_async_copy(p_in.at[index_of(n)], ps.at[n % 2], p_sem.at[n % 2])

        probs_copy(0).start()

        def close(at, gains):
            blk, half = at // 2, at % 2
            rows = pl.ds(pl.multiple_of(half * 256, 256), 256)
            h = hidden[blk, rows, :]
            r = lax.rsqrt(jnp.mean(h * h, axis=-1, keepdims=True) + EPSILON)
            d = back[blk, rows, :]
            scaled = gain_f[...] * d
            inner = jnp.mean(h * scaled, axis=-1, keepdims=True)
            grad = cots[blk, rows, :].astype(f32) + r * scaled - h * (r * r * r * inner)
            cots[blk, rows, :] = total[blk, rows, :].astype(bf16)
            hidden[blk, rows, :] = grad
            low_grad = grad.astype(bf16)
            dcs[blk, rows, :] = nt(low_grad, wo[...]).astype(bf16)
            return gains + jnp.sum(d * h * r, axis=0, keepdims=True)

        gains = lax.fori_loop(0, 4, close, jnp.zeros((1, D), f32))
        for m in range(6):
            small[0, 22 + m : 23 + m, :] = gains[:, TILE * m : TILE * m + TILE]
        for blk in range(OWN):
            start_back(cots, output, blk, 0)
        advance(1)
        advance(0)
        for copy in more:
            copy.wait()
        loads[4].wait()

        low, high = head_masks()
        corner = lax.broadcasted_iota(jnp.int32, (TILE, TILE), 0) + lax.broadcasted_iota(jnp.int32, (TILE, TILE), 1)
        flip = (corner == TILE - 1).astype(f32)
        for group in range(3):
            for side in range(2):
                pair = group + 3 * side
                lanes = slice(TILE * pair, TILE * pair + TILE)
                acc[...] = jnp.zeros_like(acc)

                def one(blk, carry):
                    n = 4 * group + 2 * side + blk
                    slot = n % 2
                    probs_copy(n).wait()

                    @pl.when(n + 1 < OWN * PAIRS)
                    def _():
                        probs_copy(n + 1).start()

                    q, k, v, dc = qs[blk, :, lanes], ks[blk, :, lanes], vs[blk, :, lanes], dcs[blk, :, lanes]
                    dq = dk = dv = None
                    for e, sel in enumerate((low, high)):
                        dce = dc * sel
                        grads = nt(v, dce)
                        for qt in range(4):
                            at_q = slice(TILE * qt, TILE * qt + TILE)
                            probs = [ps[slot, e, TILE * kt : TILE * kt + TILE, at_q].astype(f32) for kt in range(4)]
                            parts = [probs[kt] * grads[TILE * kt : TILE * kt + TILE, at_q] for kt in range(4)]
                            delta = jnp.sum(parts[0] + parts[1] + parts[2] + parts[3], axis=0, keepdims=True)
                            for kt in range(4):
                                ds = parts[kt] - probs[kt] * delta
                                acc[e, min(max(kt - qt, -2), 2) + 2] += ds
                                dsb[e, TILE * kt : TILE * kt + TILE, at_q] = ds.astype(bf16)
                        terms = (tn(dsb[e], k * sel), nn(dsb[e], q * sel), nn(ps[slot, e], dce))
                        if e == 0:
                            dq, dk, dv = terms
                        else:
                            dq, dk, dv = dq + terms[0], dk + terms[1], dv + terms[2]
                    qs[blk, :, lanes] = dq.astype(bf16)
                    ks[blk, :, lanes] = dk.astype(bf16)
                    vs[blk, :, lanes] = dv.astype(bf16)
                    return carry

                lax.fori_loop(0, OWN, one, 0)
                for e in range(2):
                    sums = []
                    for tile in range(3):
                        turned = jnp.dot(flip, acc[e, 1 + tile], preferred_element_type=f32, precision=lax.Precision.HIGHEST)
                        wide = jnp.concatenate([turned, jnp.zeros((TILE, TILE), f32)], axis=1)
                        wide = pltpu.roll(wide, 0, 1, stride=1, stride_axis=0)
                        sums.append(jnp.sum(wide, axis=0, keepdims=True))
                    buckets_acc[2 * pair + e : 2 * pair + e + 1, 0:768] = jnp.concatenate(sums, axis=1)
                    buckets_acc[2 * pair + e : 2 * pair + e + 1, 768:896] = jnp.sum(acc[e, 0], axis=0, keepdims=True)
                    buckets_acc[2 * pair + e : 2 * pair + e + 1, 896:1024] = jnp.sum(acc[e, 4], axis=0, keepdims=True)
                if side == 0:
                    if group == 0:
                        advance(2), advance(1), advance(0)
                    elif group == 1:
                        advance(2), advance(1), advance(0), advance(3)
                    else:
                        advance(2), advance(1), advance(4), advance(3)
            for side in range(2):
                pair = group + 3 * side
                lanes = slice(TILE * pair, TILE * pair + TILE)
                qk = tn(flat(ns), jnp.concatenate([flat(t, lanes) for t in (qs, ks)], axis=1)).astype(bf16)
                grad_v = tn(flat(ns), flat(vs, lanes)).astype(bf16)
                grad_o = tn(flat(cs), flat(hidden, lanes).astype(bf16)).astype(bf16)
                pieces = ((qk[:, :TILE], qk[:, TILE:]), (grad_v, grad_o))
                base = ffn_base(group, 1 - c)
                for kind in range(2):
                    for half in range(2):
                        own[base + 2 * half + kind, :, :, :, side] = pieces[kind][half].reshape(2, 2, 2, 96, TILE)
            item = STEPS + group
            advance(item)
            if group == 0:
                advance(2), advance(1), advance(0)
            elif group == 1:
                advance(2), advance(3), advance(1), advance(0)
            else:
                advance(5), advance(4), advance(3), advance(2)


        def first_norm(at, gains):
            blk, half = at // 2, at % 2
            rows = pl.ds(pl.multiple_of(half * 256, 256), 256)
            d = nt(qs[blk, rows, :], wq[...]) + nt(ks[blk, rows, :], wk[...]) + nt(vs[blk, rows, :], wv[...])
            h = xs[blk, rows, :].astype(f32)
            r = lax.rsqrt(jnp.mean(h * h, axis=-1, keepdims=True) + EPSILON)
            scaled = gain_a[...] * d
            inner = jnp.mean(h * scaled, axis=-1, keepdims=True)
            xs[blk, rows, :] = (hidden[blk, rows, :] + r * scaled - h * (r * r * r * inner)).astype(bf16)
            return gains + jnp.sum(d * h * r, axis=0, keepdims=True)

        gains = lax.fori_loop(0, 2, first_norm, jnp.zeros((1, D), f32))
        start_back(xs, grad_tokens, 0, 1)
        advance(5), advance(4), advance(3)
        gains = lax.fori_loop(2, 4, first_norm, gains)
        start_back(xs, grad_tokens, 1, 1)
        for m in range(6):
            small[0, 16 + m : 17 + m, :] = gains[:, TILE * m : TILE * m + TILE]

    pl.run_scoped(
        attention,
        qs=pltpu.VMEM((OWN, BLOCK, D), bf16),
        ks=pltpu.VMEM((OWN, BLOCK, D), bf16),
        vs=pltpu.VMEM((OWN, BLOCK, D), bf16),
        ps=pltpu.VMEM((2, 2, BLOCK, BLOCK), bf16),
        dsb=pltpu.VMEM((2, BLOCK, BLOCK), bf16),
        acc=pltpu.VMEM((2, 5, TILE, TILE), f32),
        wq=pltpu.VMEM((D, D), bf16),
        wk=pltpu.VMEM((D, D), bf16),
        wv=pltpu.VMEM((D, D), bf16),
        l_sem=DMA((6,)),
        p_sem=DMA((2,)),
    )

    lane = lax.broadcasted_iota(jnp.int32, (1, 2 * TILE), 1)
    offsets = jnp.concatenate([TILE * tile + TILE - 1 - lane for tile in (-1, 0, 1)], axis=1)
    far = lax.broadcasted_iota(jnp.int32, (1, 256), 1)
    column = jnp.concatenate([bucket_of(offsets), jnp.where(far < TILE, 15, 31)], axis=1)
    hot = (lax.broadcasted_iota(jnp.int32, (TILE, 1024), 0) == column).astype(f32)
    small[0, 0:16, :] = lax.dot_general(
        buckets_acc[...], hot, (((1,), (1,)), ((), ())), preferred_element_type=f32, precision=lax.Precision.HIGHEST
    )
    for at, axis in enumerate(("c", "y", "x", "z0", "z1")):
        copy = remote(small.at[at], small_in.at[at], sm_send.at[at], sm_recv.at[at], partner[axis])
        copy.start()
        if at < 4:
            for item in range(6):
                if state[item] < 7:
                    advance(item)
        copy.wait()
        if at < 4:
            small[at + 1] = small[at] + small_in[at]
        else:
            g_small[...] = small[at] + small_in[at]
    while any(state[item] < 7 for item in range(6)):
        for item in range(6):
            if state[item] < 7:
                advance(item)
    wait_back(cots, output, 0)
    wait_back(xs, grad_tokens, 1)
    emit(c, f_ffn, rf_ffn, f_att, rf_att, g_qkvo, g_in, g_back)


def emit(c, f_ffn, rf_ffn, f_att, rf_att, g_qkvo, g_in, g_back):
    first = c == 0
    for step in range(STEPS):
        for b in range(2):
            kept, got = f_ffn[step, c, b].astype(f32), rf_ffn[step, b].astype(f32)
            g_in[:, 384 * b + TILE * step : 384 * b + TILE * step + TILE] = jnp.where(first, kept, got)
            g_back[TILE * step : TILE * step + TILE, 96 * b : 96 * b + 96] = jnp.where(first, got, kept).T
    for half in range(2):
        for kind in range(2):
            pieces = []
            for g in range(3):
                kept, got = f_att[g, half].astype(f32), rf_att[g, half].astype(f32)
                pieces.append(jnp.where(first, kept, got) if kind == 0 else jnp.where(first, got, kept))
            wide = jnp.concatenate(pieces, axis=1)
            at = 2 * kind + half
            g_qkvo[at] = jnp.where(first, wide[:, :192], wide[:, 192:])


def rest_call(outer, x, cot, n, q, k, v, ctx, probs, w_q, w_k, w_v, w_o, w_in, w_back, gain_a, gain_f):
    rows = (OWN, BLOCK, D)
    local = jax.ShapeDtypeStruct((ROWS, TILE, D), bf16)
    halves = (3, 2)
    scratch = [
        pltpu.VMEM(rows, bf16),
        pltpu.VMEM(rows, bf16),
        pltpu.VMEM(rows, bf16),
        pltpu.VMEM(rows, bf16),
        pltpu.VMEM(rows, f32),
        pltpu.VMEM(rows, f32),
        pltpu.VMEM(rows, f32),
        pltpu.VMEM(rows, bf16),
        pltpu.VMEM((D, D), bf16),
        pltpu.VMEM((24,) + UNIT, bf16),
        pltpu.VMEM((3, 4) + UNIT, bf16),
        pltpu.VMEM((3, 2) + UNIT, bf16),
    ]
    for dims in ((2,), ()):
        for stage in range(4):
            scratch.append(pltpu.VMEM(halves + dims + (2,) * (3 - stage) + UNIT[4:], bf16))
    scratch += [
        pltpu.VMEM((3, 2, 2) + UNIT[4:], bf16),
        pltpu.VMEM((3, 2) + UNIT[4:], bf16),
        pltpu.VMEM((3, 2) + UNIT[4:], bf16),
        pltpu.VMEM((3, 2) + UNIT[4:], bf16),
        pltpu.VMEM((5, 32, TILE), f32),
        pltpu.VMEM((5, 32, TILE), f32),
        pltpu.VMEM((16, 1024), f32),
        DMA((5,)), DMA((3,)), DMA((3,)), DMA((3, 2)), DMA((3, 2)),
        DMA((6, 2, 4)), DMA((6, 2, 4)), DMA((6,)), DMA((6,)), DMA((5,)), DMA((5,)),
        DMA((2, OWN)), DMA((2, OWN, 3)), DMA((2, OWN, 3)),
    ]
    return pl.pallas_call(
        functools.partial(rest_kernel, outer),
        out_shape=(
            local,
            local,
            jax.ShapeDtypeStruct((4, 96, 192), f32),
            jax.ShapeDtypeStruct((96, D), f32),
            jax.ShapeDtypeStruct((384, 192), f32),
            jax.ShapeDtypeStruct((32, TILE), f32),
        ),
        in_specs=[ANY] * 14 + [VMEM, VMEM],
        out_specs=(ANY, ANY, VMEM, VMEM, VMEM, VMEM),
        scratch_shapes=scratch,
        compiler_params=pltpu.CompilerParams(collective_id=1, has_side_effects=True, vmem_limit_bytes=63 * 2**20),
    )(x, cot, n, q, k, v, ctx, probs, w_q, w_k, w_v, w_o, w_in, w_back, gain_a, gain_f)


def shards(
    tokens, bucket_of_block, lengths, w_query, w_key, w_value, w_out, w_in, w_back, gain_attn, gain_ffn, bias_table, cotangent
):
    devices = lax.axis_size("dp")
    outer = devices // 8
    gain_a, gain_f = gain_attn.reshape(1, D), gain_ffn.reshape(1, D)
    per = bias_table.shape[1]
    table = jnp.pad(bias_table.T, ((0, 8 - per), (0, TILE - BUCKETS)))
    kept = attend_call(tokens, cotangent, table, w_query, w_key, w_value, gain_a, bucket_of_block, lengths)
    output, grad_tokens, g_qkvo, g_in, g_back, g_small = rest_call(
        outer, *kept, w_query, w_key, w_value, w_out, w_in, w_back, gain_a, gain_f
    )
    weights = [g_qkvo[0], g_qkvo[1], g_qkvo[2], g_qkvo[3], g_in, g_back]
    if outer > 1:
        groups = [[at * outer + spare for spare in range(outer)] for at in range(8)]
        weights = [
            lax.psum_scatter(grad, "dp", scatter_dimension=0, axis_index_groups=groups, tiled=True) for grad in weights
        ]
        g_small = lax.psum(g_small, "dp", axis_index_groups=groups)
    me = lax.axis_index("head")
    gains = g_small[16:28].reshape(2, D)
    gains = lax.dynamic_slice(gains, (0, me * (D // GROUP)), (2, D // GROUP))
    table_grad = lax.dynamic_slice(g_small, (me * per, 0), (per, BUCKETS)).T
    return (output, grad_tokens, *weights, gains[0], gains[1], table_grad)


def solution(mesh):
    whole = P()
    rows = P("dp", "head", None)
    block = P("dp", "head")
    return jax.shard_map(
        shards,
        mesh=mesh,
        in_specs=(rows, P("dp", None), P("dp", None, None)) + (whole,) * 8 + (P(None, "head"), rows),
        out_specs=(rows, rows) + (block,) * 6 + (P("head"), P("head"), P(None, "head")),
        check_vma=False,
    )
```

time: 1180 us -> 212 us (0.18)
  waiting for transfers between devices: 513 us -> 0 us
  local copies, waits for them, and re-layouts: 229 us -> 15.4 us
  matrix products: 207 us -> 0 us
  Pallas kernels: 0 us -> 191 us
  blocking collectives: 132 us -> 0 us
  other arithmetic: 55.9 us -> 0 us
  starting transfers between devices: 22.8 us -> 0 us
  between operations: 15.4 us -> 1.12 us
    reduce_scatter x7 -> x0, waiting for transfers between devices: 404 us -> none  [the longest x1 151 us: shards(): lax.psum_scatter(grad_w_back, 'dp', scatter_dimension=0, tiled=True)]
    dot_general x76 -> x0, matrix products: 207 us -> none  [the longest x16 31.6 us: scores_of(): jnp.einsum('qhd,khd->hqk', split_heads(query_block), split_heads(key_bloc...]
    pallas_call x0 -> x2, Pallas kernels: none -> 191 us  [the longest x1 147 us: rest_call(): pl.pallas_call(functools.partial(rest_kernel, outer), out_shape=(local, l...]
    all_to_all x3 -> x0, blocking collectives: 90.9 us -> none  [the longest x1 30.4 us: shards(): lax.all_to_all(context_heads, 'head', split_axis=1, concat_axis=2, tiled=...]
    all_to_all x5 -> x0, waiting for transfers between devices: 56.5 us -> none  [the longest x1 24.1 us: shards(): lax.all_to_all(head_grads[1], 'head', split_axis=1, concat_axis=2, tiled=...]
    unnamed x17 -> x0, waiting for transfers between devices: 51.9 us -> none
    dynamic_slice x48 -> x0, local copies, waits for them, and re-layouts: 47.4 us -> none  [shards(): lax.map(attend, (head_query, head_key, head_value, valid_pairs))]
    eq x1 -> x0, local copies, waits for them, and re-layouts: 45.7 us -> none  [shards(): rel_bucket(positions[None, :] - positions[:, None])[:, :, None]]
  transfers between devices with their start and end apart: 17 -> 0, of which waited for: 12 -> 0; matrix products, arithmetic and copies ran while one was open for 29% -> 0% of each run, Pallas kernels for 0% -> 0%
where the time goes in v1:
time: 212 us; the launch traced here: 208 us
  Pallas kernels  191 us (90%)
  local copies, waits for them, and re-layouts  15.4 us (7%)
    pallas_call x1, Pallas kernels, rest_call(): pl.pallas_call(functools.partial(rest_kernel, outer), out_shape=(local, l...  147 us
    pallas_call x1, Pallas kernels, attend_call(): pl.pallas_call(attend_kernel, out_shape=(rows,) * 7 + (probs,), in_specs=...  44 us
    unnamed x11, local copies, waits for them, and re-layouts  7.84 us

profile of v1, /device:TPU:0, one launch (start us, length us, event | category | flops | bytes accessed | tf_op | source)
XLA Modules:
  0.0 208.0 jit_solution(5544065789590592537)
XLA Ops:
  0.6 1.3 reshape.31.gain.gain_a
  1.9 1.3 copy.24.lengths
  3.3 1.3 pad.4.table
  4.5 0.0 copy-start.2
  4.5 44.0 %shard_map.212 = (bf16[2,512,768]{2,1,0:T(8,128)(2,1)}, bf16[2,512,768]{2,1,0:T(8,128)(2,1)}, bf16[2,512,768]{2,1,0:T(8,128)(2,1)}, bf16[2,512,768]{2,1,0:T(8,12...) custom-call(bf16[8,128,768]{2,1,0:T(8,128)(2,1)} %tokens.1, ...), custom_call_target="tpu_custom_call" | custom-call | tf_op jit(solution)/shard_map/pallas_call | solution.py:251
  48.5 0.0 copy-done.2
  48.5 0.6 reshape.32.gain_f
  49.1 147.5 %shard_map.213 = (bf16[8,128,768]{2,1,0:T(8,128)(2,1)}, bf16[8,128,768]{2,1,0:T(8,128)(2,1)}, f32[4,96,192]{2,1,0:T(8,128)}, f32[96,768]{1,0:T(8,128)}, f32[384,192]{1,0:T(8,128)}, /*index=5*/f32[32,128]{1,0:T(8,128)}) custom-call(bf16[2,512,768]{2,1,0:T(8,128)(2,1)} %get-tuple-element.25.x_in, bf16[2,512,768]{2,1,0:T(8,128)(2,1)} %get-tuple-element.26.cot_in, ...), custom_call_target="tpu_custom_call" | custom-call | tf_op jit(solution)/shard_map/pallas_call | solution.py:806
  196.6 1.8 slice_bitcast_fusion
  198.4 0.7 slice.25
  199.1 0.6 fusion
  199.7 1.3 dynamic-slice_bitcast_fusion
  201.0 1.9 copy.25
  202.9 0.0 copy-start
  202.9 2.8 %copy.29 = bf16[8,128,768]{2,1,0:T(8,128)(2,1)} copy(bf16[8,128,768]{2,1,0:T(8,128)(2,1)} %get-tuple-element.67) | data formatting | bytes 3145728
  205.7 0.0 copy-done
  205.7 0.0 copy-start.1
  205.7 1.1 copy.30
  206.8 0.0 copy-done.1
  206.8 0.7 copy.31
  (1 shorter events, 0.0 us)
Async XLA Ops:
  4.5 44.0 %copy-start.2 = (f32[768]{0:T(1024)S(1)}, f32[768]{0:T(1024)}, u32[]{:S(2)}) copy-start(f32[768]{0:T(1024)} %param.23) | copy-start | bytes 9220
  202.9 2.8 %copy-start = (bf16[8,128,768]{2,1,0:T(8,128)(2,1)S(1)}, bf16[8,128,768]{2,1,0:T(8,128)(2,1)}, u32[]{:S(2)}) copy-start(bf16[8,128,768]{2,1,0:T(8,128)(2,1)} %get-tuple-element.68) | copy-start | bytes 4718596
  205.7 1.1 copy-start.1
